TPU v7x, 512 devices: a whole 4x8x8 slice. The times are simulated.
512 devices in a mesh: row: 16 (over y, core), col: 16 (over z, x_hi), bin: 2 (over x_lo).
Axes of the slice: x: 4 (x_hi: 2, x_lo: 2; x = x_hi * 2 + x_lo), y: 8, z: 8, core: 2. Of those that a mesh axis runs over, the one named last changes fastest.
Arguments:
- records: bfloat16 [4096, 26624], P('row', 'col'), may hold values from -400 to 400
- offsets: int32 [16], P('col'), may hold values from 0 to 164, as said below
- live_flags: int32 [4096], P('row'), may hold values 0 or 1
Outputs:
- cross_spectra: bfloat16 [32, 2, 4096, 4096], P('bin', None, 'row', 'col')
Inputs may be any that keep to these rules, and one draw needn't show every extreme that they name: `offsets`: some window has delay 0 and some has delay 164.
All inputs are finite; a program needn't handle non-finite values. No bound on the sum of `live_flags` on one device may be relied on, other than what follows from the above.
Results may differ from a plain program's by a relative error of at most 0.007.
Values sent between devices are 32-bit elements; how exact they have to be, the bound alone decides.
A program may use at most 64 MiB of HBM per device.

v0:
```python
import math

import jax
import jax.numpy as jnp
from jax import lax
from jax.sharding import PartitionSpec as P

L = 1500
NB = 32
BSTEP = 6


epsilon = 1e-05


def broadcast(block, axis, holder):
    block = jnp.where(lax.axis_index(axis) == holder, block, jnp.zeros_like(block))
    return lax.psum(block, axis)


def make_table(first_bin, bin_count, length, stride):
    bin_ids = (first_bin + lax.iota(jnp.int32, bin_count) + 1) * stride
    sample_ids = lax.iota(jnp.int32, length)
    angles = (bin_ids[:, None] * sample_ids[None, :] % length).astype(jnp.float32) * (
        2.0 * math.pi / length
    )
    tapering = 0.5 - 0.5 * jnp.cos(sample_ids.astype(jnp.float32) * (2.0 * math.pi / length))
    return jnp.stack([jnp.cos(angles) * tapering, -jnp.sin(angles) * tapering]).astype(jnp.bfloat16)


def spectra_of(records, offsets, dft_table):
    bin_count = dft_table.shape[1]
    length = dft_table.shape[2]
    flat_table = dft_table.reshape(2 * bin_count, length)
    segment = lax.dynamic_slice_in_dim(records, 0 + offsets[0], length, 1)
    product = lax.dot_general(
        flat_table, segment, (((1,), (1,)), ((), ())), preferred_element_type=jnp.float32
    )
    spectra_list = [product.reshape(2, bin_count, records.shape[0])]
    return jnp.stack(spectra_list)


def combine_block(right_block):
    turned = jnp.stack([-right_block[:, 1], right_block[:, 0]], axis=1)
    return jnp.stack([right_block, turned], axis=2)


def stack_terms(left_block, paired):
    return jnp.einsum(
        "wpfc,wpqfd->fqcd",
        left_block,
        paired,
        precision=lax.Precision.HIGHEST,
        preferred_element_type=jnp.float32,
    )


def per_device(records, offsets, live_flags):
    per_half = NB // lax.axis_size("bin")
    bin_index = lax.axis_index("bin")
    spectra = spectra_of(records, offsets, make_table(bin_index * per_half, per_half, L, BSTEP))
    energy = lax.psum(jnp.sum(spectra * spectra, axis=(1, 2)), "bin") / (2 * NB)
    scaling = live_flags.astype(jnp.float32) / jnp.sqrt(energy + epsilon)
    whitened = spectra * scaling[:, None, None, :]
    windows = whitened.shape[0] * lax.axis_size("col")
    own_block = lax.all_gather(whitened, "col", axis=0, tiled=True)
    mirror_rows = broadcast(own_block, "row", lax.axis_index("col"))
    stacked = stack_terms(own_block, combine_block(mirror_rows))
    return (stacked / windows).astype(jnp.bfloat16)


def solution(mesh):
    in_specs = (P("row", "col"), P("col"), P("row"))
    out_specs = P("bin", None, "row", "col")
    return jax.shard_map(
        per_device, mesh=mesh, in_specs=in_specs, out_specs=out_specs, check_vma=False
    )
```

profile of v0, /device:TPU:1, one launch (start us, length us, event | category | flops | bytes accessed | tf_op | source)
XLA Modules:
  0.0 199.1 jit_solution(1383178437781744687)
XLA Ops:
  6.5 0.0 copy-start
  6.5 0.0 all-reduce.2.cloned.1.call-start
  6.5 0.1 multiply_subtract_fusion
  7.3 0.7 convert_element_type.40
  8.0 0.5 multiply_convert_fusion.1
  8.5 0.0 copy-done
  8.5 0.4 multiply_reduce_fusion
  9.0 4.4 %psum.14 = f32[1,256]{1,0:T(1,128)S(1)} all-reduce(f32[1,256]{1,0:T(1,128)S(1)} %bitcast.31), channel_id=1, replica_groups=mesh['row'=16,'col'=16,'bin'=2] {'bin'}, use_global_device_ids=true, to_apply=%region_1.2 | all-reduce | flops 256 | bytes 2048 | tf_op jit(solution)/shard_map/psum | solution.py:62
  13.4 42.9 %all_gather.3 = f32[16,2,16,256]{3,2,1,0:T(8,128)S(1)} all-gather(f32[1,2,16,256]{3,2,1,0:T(8,128)S(1)} %broadcast_multiply_fusion), channel_id=1, replica_groups=mesh['row'=16,'col'=16,'bin'=2] {'col'}, dimensions={0}, use_global_device_ids=true | all-gather | bytes 557056 | tf_op jit(solution)/shard_map/all_gather | solution.py:66
  56.3 1.1 copy_select_fusion
  57.4 0.0 all-reduce.2.cloned.1.call-update
  57.5 117.9 %all-reduce.2.cloned.1.call-done = f32[16,2,16,256]{3,0,1,2:T(8,128)} async-done(((f32[16,2,16,256]{3,0,1,2:T(8,128)}), f32[16,2,16,256]{3,0,1,2:T(8,128)}) %all-reduce.2.cloned.1.call-update) | async-done | bytes 524304 | tf_op jit(solution)/shard_map/psum | solution.py:18
  175.4 1.1 slice_negate_fusion
  176.5 9.4 %fusion.1 = bf16[16,2,256,256]{2,3,1,0:T(8,128)(2,1)} fusion(f32[16,2,1,16,256]{4,0,1,2,3:T(8,128)S(1)} %maximum_bitcast_fusion, f32[16,2,1,16,256]{4,0,1,2,3:T(8,128)} %bitcast.26, f32[16,2,16,256,1]{3,2,1,0,4:T(8,128)S(1)} %bitcast.25), kind=kOutput, calls=%fused_computation.2 | convolution fusion | flops 809762816 | bytes 5767168 | tf_op jit(solution)/shard_map/wpfc,wpqfd->fqcd/dot_general | solution.py:49
  185.9 6.4 %copy.10 = bf16[16,2,256,256]{3,2,1,0:T(8,128)(2,1)} copy(bf16[16,2,256,256]{2,3,1,0:T(8,128)(2,1)} %fusion.1) | data formatting | bytes 8388608 | tf_op jit(solution)/shard_map/convert_element_type | solution.py:69
  (5 shorter events, 0.1 us)
Async XLA Ops:
  6.5 2.0 %copy-start = (bf16[256,1664]{1,0:T(8,128)(2,1)S(1)}, bf16[256,1664]{1,0:T(8,128)(2,1)}, u32[]{:S(2)}) copy-start(bf16[256,1664]{1,0:T(8,128)(2,1)} %param.3) | copy-start | bytes 2555908
  6.5 168.8 %all-reduce.2.cloned.1.call-start = ((), (), s32[]{:S(2)}) async-start(), calls=%async_computation | async-start | bytes 1048576 | tf_op jit(solution)/shard_map/psum | solution.py:18
Sparse Core Ops, SparseCore 0:
  57.6 117.7 all-reduce.1
where the time goes:
time: 199 us
  waiting for transfers between devices  118 us (59%)
  blocking collectives  47.3 us (24%)
  between operations  14.2 us (7%)
  matrix products  9.83 us (5%)
  local copies, waits for them, and re-layouts  6.39 us (3%)
  other arithmetic  3.5 us (2%)
    psum x1, waiting for transfers between devices, broadcast(): return lax.psum(block, axis)  118 us
    all_gather x1, blocking collectives, per_device(): own_block = lax.all_gather(whitened, 'col', axis=0, tiled=True)  42.9 us
    dot_general x1, matrix products, stack_terms(): jnp.einsum('wpfc,wpqfd->fqcd', left_block, paired, precision=lax.Precisio...  9.38 us
    convert_element_type x1, local copies, waits for them, and re-layouts, per_device(): return (stacked / windows).astype(jnp.bfloat16)  6.38 us
    psum x1, blocking collectives, per_device(): energy = lax.psum(jnp.sum(spectra * spectra, axis=(1, 2)), 'bin') / (2 * NB)  4.35 us
  transfers between devices with their start and end apart: 1, of which 1 were waited for; matrix products, arithmetic and copies ran while one was open for 0% of the time, Pallas kernels for 0%

commit v1 on v0

v1 whole, which is shorter than its diff:
```python
import math

import jax
import jax.numpy as jnp
import numpy as np
from jax import lax
from jax.experimental import pallas as pl
from jax.experimental.pallas import tpu as pltpu
from jax.sharding import PartitionSpec as P

L = 1500
NB = 32
BSTEP = 6
EPSILON = 1e-05
MESH = pl.DeviceIdType.MESH
SLOT = 64
WINDOWS = 16
NEAR_FIRST = (1, 7, 2, 6, 3, 5, 4)


def dft_rows():
    bins = (np.arange(NB) + 1) * BSTEP
    samples = np.arange(L)
    angles = (bins[:, None] * samples[None, :] % L) * (2.0 * math.pi / L)
    taper = 0.5 - 0.5 * np.cos(samples * (2.0 * math.pi / L))
    rows = np.stack([np.cos(angles) * taper, -np.sin(angles) * taper], axis=1)
    return jnp.asarray(rows.reshape(2 * NB, L).astype(np.float32)).astype(jnp.bfloat16)


def gather_kernel(spectra_ref, live_ref, left_ref, right_ref, send_sem, left_sem, right_sem):
    row, col, half = lax.axis_index("row"), lax.axis_index("col"), lax.axis_index("bin")
    y, core = row // 2, row % 2
    z, side = col // 2, col % 2

    def device(y, core, z, side):
        return (y * 2 + core, z * 2 + side, half)

    def along(step):
        return lax.rem(z + step, 8)

    barrier = pltpu.get_barrier_semaphore()
    partners = [device(y, core, along(i), side) for i in range(1, 8)]
    partners += [device(y, core, z, 1 - side), device(y, 1 - core, z, side)]
    for target in partners:
        pl.semaphore_signal(barrier, inc=1, device_id=target, device_id_type=MESH)
    for i in range(8):
        pl.semaphore_signal(
            barrier, inc=1, device_id=device(z, side, i, core), device_id_type=MESH
        )

    spectra = spectra_ref[...]
    energy = jnp.sum(spectra * spectra, axis=0, keepdims=True) / (2 * NB)
    scaling = live_ref[...].astype(jnp.float32) * lax.rsqrt(energy + EPSILON)
    mine = spectra_ref[pl.ds(pl.multiple_of(half * NB, NB), NB), :] * scaling
    left_ref[col, 0:32, :] = mine[:, :128]
    left_ref[col, 32:64, :] = mine[:, 128:]

    pl.semaphore_wait(barrier, 17)

    sent = []

    def send(source, target_ref, sem, device_id):
        copy = pltpu.make_async_remote_copy(
            src_ref=source,
            dst_ref=target_ref,
            send_sem=send_sem.at[len(sent)],
            recv_sem=sem,
            device_id=device_id,
            device_id_type=MESH,
        )
        sent.append(copy)
        return copy

    def wait_for(ref, sem, slot):
        pltpu.make_async_copy(ref.at[slot], ref.at[slot], sem.at[slot]).wait()

    own = left_ref.at[col]
    send(own, own, left_sem.at[col], device(y, core, z, 1 - side)).start()
    for i in NEAR_FIRST:
        send(own, own, left_sem.at[col], device(y, core, along(i), side)).start()
    for j in (1, 7, 2, 6, 3, 5, 4):
        send(
            own, right_ref.at[col], right_sem.at[col], device(lax.rem(y + j, 8), side, y, core)
        ).start()
    stays = jnp.logical_and(z == y, side == core)
    keep = pltpu.make_async_copy(own, right_ref.at[col], right_sem.at[col])
    move = send(own, right_ref.at[col], right_sem.at[col], device(y, side, y, core))

    @pl.when(stays)
    def _():
        keep.start()

    @pl.when(jnp.logical_not(stays))
    def _():
        move.start()

    for i in (0,) + NEAR_FIRST:
        if i:
            slot = along(i) * 2 + side
            wait_for(left_ref, left_sem, slot)
            block = left_ref.at[slot]
            send(block, block, left_sem.at[slot], device(y, core, z, 1 - side)).start()
        slot = along(i) * 2 + core
        wait_for(right_ref, right_sem, slot)
        block = right_ref.at[slot]
        send(block, block, right_sem.at[slot], device(y, 1 - core, z, side)).start()
    for i in (0,) + NEAR_FIRST:
        wait_for(left_ref, left_sem, along(i) * 2 + 1 - side)
        wait_for(right_ref, right_sem, along(i) * 2 + 1 - core)
    for copy in sent:
        if copy is not move:
            copy.wait_send()

    @pl.when(jnp.logical_not(stays))
    def _():
        move.wait_send()


def stack_kernel(left_ref, right_ref, out_ref):
    step = pl.program_id(0)
    for k in range(out_ref.shape[0]):
        first = (step * out_ref.shape[0] + k) * 2

        def rows(ref, part):
            return jnp.concatenate(
                [ref[pl.ds(first + part + h * 32, WINDOWS, stride=SLOT), :] for h in (0, 1)],
                axis=1,
            )

        real, imag = rows(right_ref, 0), rows(right_ref, 1)
        left = jnp.concatenate([rows(left_ref, 0), rows(left_ref, 1)], axis=0)
        left = left.astype(jnp.bfloat16)
        straight = jnp.concatenate([real, imag], axis=0).astype(jnp.bfloat16)
        turned = jnp.concatenate([-imag, real], axis=0).astype(jnp.bfloat16)
        for part, other in enumerate((straight, turned)):
            total = lax.dot_general(
                left, other, (((0,), (0,)), ((), ())), preferred_element_type=jnp.float32
            )
            out_ref[k, part] = (total * (1.0 / WINDOWS)).astype(out_ref.dtype)


def per_device(records, offsets, live_flags):
    segment = lax.dynamic_slice_in_dim(records, offsets[0], L, 1)
    spectra = lax.dot_general(
        dft_rows(), segment, (((1,), (1,)), ((), ())), preferred_element_type=jnp.float32
    )
    channels = records.shape[0]
    vmem = pl.BlockSpec(memory_space=pltpu.VMEM)
    gathered = jax.ShapeDtypeStruct((WINDOWS, SLOT, channels // 2), jnp.float32)
    left, right = pl.pallas_call(
        gather_kernel,
        out_shape=(gathered, gathered),
        in_specs=[vmem, vmem],
        out_specs=(vmem, vmem),
        scratch_shapes=[
            pltpu.SemaphoreType.DMA((31,)),
            pltpu.SemaphoreType.DMA((WINDOWS,)),
            pltpu.SemaphoreType.DMA((WINDOWS,)),
        ],
        compiler_params=pltpu.CompilerParams(
            collective_id=0, has_side_effects=True, vmem_limit_bytes=8 * 2**20
        ),
        name="gather_spectra",
    )(spectra, live_flags.reshape(1, channels))
    left = left.reshape(WINDOWS * SLOT, channels // 2)
    right = right.reshape(WINDOWS * SLOT, channels // 2)
    per_step = 4
    return pl.pallas_call(
        stack_kernel,
        grid=(16 // per_step,),
        out_shape=jax.ShapeDtypeStruct((16, 2, channels, channels), jnp.bfloat16),
        in_specs=[vmem, vmem],
        out_specs=pl.BlockSpec((per_step, 2, channels, channels), lambda i: (i, 0, 0, 0)),
        compiler_params=pltpu.CompilerParams(vmem_limit_bytes=16 * 2**20),
        name="stack_windows",
    )(left, right)


def solution(mesh):
    in_specs = (P("row", "col"), P("col"), P("row"))
    out_specs = P("bin", None, "row", "col")
    return jax.shard_map(
        per_device, mesh=mesh, in_specs=in_specs, out_specs=out_specs, check_vma=False
    )
```

time: 199 us -> 37.8 us (0.19)
  waiting for transfers between devices: 118 us -> 0 us
  blocking collectives: 47.3 us -> 0 us
  Pallas kernels: 0 us -> 34.2 us
  between operations: 14.2 us -> 0.76 us
  matrix products: 9.83 us -> 1.37 us
  local copies, waits for them, and re-layouts: 6.39 us -> 1.11 us
  other arithmetic: 3.5 us -> 0 us
    psum x1 -> x0, waiting for transfers between devices: 118 us -> none  [broadcast(): return lax.psum(block, axis)]
    all_gather x1 -> x0, blocking collectives: 42.9 us -> none  [per_device(): own_block = lax.all_gather(whitened, 'col', axis=0, tiled=True)]
    pallas_call x0 -> x2, Pallas kernels: none -> 34.2 us  [the longest x1 30.8 us: per_device(): pl.pallas_call(gather_kernel, out_shape=(gathered, gathered), in_specs=[v...]
    dot_general x2 -> x1, matrix products: 9.83 us -> 1.37 us  [per_device(): lax.dot_general(dft_rows(), segment, (((1,), (1,)), ((), ())), preferred_...]
    convert_element_type x1 -> x0, local copies, waits for them, and re-layouts: 6.38 us -> none  [per_device(): return (stacked / windows).astype(jnp.bfloat16)]
    psum x1 -> x0, blocking collectives: 4.35 us -> none  [per_device(): energy = lax.psum(jnp.sum(spectra * spectra, axis=(1, 2)), 'bin') / (2 * NB)]
  transfers between devices with their start and end apart: 1 -> 0, of which waited for: 1 -> 0; matrix products, arithmetic and copies ran while one was open for 0% -> 0% of each run, Pallas kernels for 0% -> 0%
where the time goes in v1:
time: 37.8 us; the launch traced here: 37.5 us
  Pallas kernels  34.2 us (90%)
  matrix products  1.37 us (4%)
  local copies, waits for them, and re-layouts  1.11 us (3%)
  between operations  0.76 us (2%)
    pallas_call x1, Pallas kernels, per_device(): pl.pallas_call(gather_kernel, out_shape=(gathered, gathered), in_specs=[v...  30.8 us
    pallas_call x1, Pallas kernels, per_device(): pl.pallas_call(stack_kernel, grid=(16 // per_step,), out_shape=jax.ShapeD...  3.41 us
    dot_general x1, matrix products, per_device(): lax.dot_general(dft_rows(), segment, (((1,), (1,)), ((), ())), preferred_...  1.37 us
    unnamed x4, local copies, waits for them, and re-layouts  1.11 us

profile of v1, /device:TPU:1, one launch (start us, length us, event | category | flops | bytes accessed | tf_op | source)
XLA Modules:
  0.0 37.5 jit_solution(12807861073537263827)
XLA Ops:
  0.0 0.0 copy-start
  0.7 0.4 %copy-done = bf16[256,1664]{1,0:T(8,128)(2,1)S(1)} copy-done((bf16[256,1664]{1,0:T(8,128)(2,1)S(1)}, bf16[256,1664]{1,0:T(8,128)(2,1)}, u32[]{:S(2)}) %copy-start) | copy-done | bytes 851992
  1.2 1.4 %fusion.spectra_ref = f32[64,256]{1,0:T(8,128)S(1)} fusion(bf16[64,1500]{1,0:T(8,128)(2,1)} %constant.8, bf16[256,1664]{1,0:T(8,128)(2,1)S(1)} %copy-done, s32[]{:T(128)S(6)} %select_n.3), kind=kOutput, calls=%fused_computation | convolution fusion | flops 49152000 | bytes 1043972 | tf_op jit(solution)/shard_map/dot_general | solution.py:144
  2.6 0.0 copy-start.1
  2.6 0.7 %copy-done.1 = s32[256]{0:T(256)S(1)} copy-done((s32[256]{0:T(256)S(1)}, s32[256]{0:T(256)}, u32[]{:S(2)}) %copy-start.1) | copy-done | bytes 1048
  3.2 30.8 %gather_spectra.1 = (f32[16,64,128]{2,1,0:T(8,128)S(1)}, f32[16,64,128]{2,1,0:T(8,128)S(1)}) custom-call(f32[64,256]{1,0:T(8,128)S(1)} %fusion.spectra_ref, s32[1,256]{1,0:T(1,128)S(1)} %bitcast.10), custom_call_target="tpu_custom_call" | custom-call | tf_op jit(solution)/shard_map/gather_spectra/pallas_call | solution.py:150
  34.1 3.4 %stack_windows.1 = bf16[16,2,256,256]{3,2,1,0:T(8,128)(2,1)} custom-call(f32[1024,128]{1,0:T(8,128)S(1)} %bitcast.8, f32[1024,128]{1,0:T(8,128)S(1)} %bitcast.9), custom_call_target="tpu_custom_call" | custom-call | tf_op jit(solution)/shard_map/stack_windows/pallas_call | solution.py:168
Async XLA Ops:
  0.0 1.2 %copy-start = (bf16[256,1664]{1,0:T(8,128)(2,1)S(1)}, bf16[256,1664]{1,0:T(8,128)(2,1)}, u32[]{:S(2)}) copy-start(bf16[256,1664]{1,0:T(8,128)(2,1)} %param.4) | copy-start | bytes 2555908
  2.6 0.7 %copy-start.1 = (s32[256]{0:T(256)S(1)}, s32[256]{0:T(256)}, u32[]{:S(2)}) copy-start(s32[256]{0:T(256)} %param.6) | copy-start | bytes 3076

commit v2 on v1

--- a/solution.py
+++ b/solution.py
@@ -18,16 +18,20 @@
 NEAR_FIRST = (1, 7, 2, 6, 3, 5, 4)
 
 
-def dft_rows():
+def dft_rows(samples_held):
     bins = (np.arange(NB) + 1) * BSTEP
     samples = np.arange(L)
     angles = (bins[:, None] * samples[None, :] % L) * (2.0 * math.pi / L)
     taper = 0.5 - 0.5 * np.cos(samples * (2.0 * math.pi / L))
     rows = np.stack([np.cos(angles) * taper, -np.sin(angles) * taper], axis=1)
-    return jnp.asarray(rows.reshape(2 * NB, L).astype(np.float32)).astype(jnp.bfloat16)
-
-
-def gather_kernel(spectra_ref, live_ref, left_ref, right_ref, send_sem, left_sem, right_sem):
+    rows = jnp.asarray(rows.reshape(2 * NB, L).astype(np.float32)).astype(jnp.bfloat16)
+    return jnp.pad(rows.astype(jnp.float32), ((0, 0), (0, samples_held - L)))
+
+
+def gather_kernel(
+    records_hbm, table_hbm, offsets_hbm, live_hbm, left_ref, right_ref,
+    records_ref, table_ref, offsets_ref, live_ref, load_sem, send_sem, left_sem, right_sem,
+):
     row, col, half = lax.axis_index("row"), lax.axis_index("col"), lax.axis_index("bin")
     y, core = row // 2, row % 2
     z, side = col // 2, col % 2
@@ -35,27 +39,62 @@
     def device(y, core, z, side):
         return (y * 2 + core, z * 2 + side, half)
 
+    def up(step):
+        return lax.rem(y + step, 8)
+
     def along(step):
         return lax.rem(z + step, 8)
 
+    parity = lax.rem(y + z, 2)
+    diagonal = jnp.logical_and(z == y, side == core)
+
     barrier = pltpu.get_barrier_semaphore()
-    partners = [device(y, core, along(i), side) for i in range(1, 8)]
-    partners += [device(y, core, z, 1 - side), device(y, 1 - core, z, side)]
-    for target in partners:
+
+    def greet(target):
         pl.semaphore_signal(barrier, inc=1, device_id=target, device_id_type=MESH)
-    for i in range(8):
-        pl.semaphore_signal(
-            barrier, inc=1, device_id=device(z, side, i, core), device_id_type=MESH
-        )
-
-    spectra = spectra_ref[...]
+
+    for i in NEAR_FIRST:
+        greet(device(y, core, along(i), side))
+    greet(device(y, core, z, 1 - side))
+    greet(device(y, 1 - core, z, side))
+    for step in (1, 7):
+        for k in range(2):
+            greet(device(up(step), k, z, side))
+    for i in range(4):
+        source = parity + 2 * i
+        own_window = jnp.logical_and(diagonal, source == z)
+        pl.when(jnp.logical_not(own_window))(
+            lambda source=source: greet(device(z, side, source, core))
+        )
+
+    loads = [
+        pltpu.make_async_copy(source, target, load_sem.at[i])
+        for i, (source, target) in enumerate(
+            (
+                (offsets_hbm, offsets_ref),
+                (table_hbm, table_ref),
+                (records_hbm, records_ref),
+                (live_hbm, live_ref),
+            )
+        )
+    ]
+    for load in loads:
+        load.start()
+    for load in loads:
+        load.wait()
+    table = pltpu.roll(table_ref[...], offsets_ref[0], 1).astype(jnp.bfloat16)
+    spectra = lax.dot_general(
+        table, records_ref[...], (((1,), (1,)), ((), ())), preferred_element_type=jnp.float32
+    )
     energy = jnp.sum(spectra * spectra, axis=0, keepdims=True) / (2 * NB)
     scaling = live_ref[...].astype(jnp.float32) * lax.rsqrt(energy + EPSILON)
-    mine = spectra_ref[pl.ds(pl.multiple_of(half * NB, NB), NB), :] * scaling
+    whitened = spectra * scaling
+    mine = jnp.where(half == 0, whitened[:NB], whitened[NB:])
     left_ref[col, 0:32, :] = mine[:, :128]
     left_ref[col, 32:64, :] = mine[:, 128:]
 
-    pl.semaphore_wait(barrier, 17)
+    self_sends = jnp.logical_and(diagonal, parity == lax.rem(y, 2))
+    pl.semaphore_wait(barrier, 17 - self_sends.astype(jnp.int32))
 
     sent = []
 
@@ -78,42 +117,47 @@
     send(own, own, left_sem.at[col], device(y, core, z, 1 - side)).start()
     for i in NEAR_FIRST:
         send(own, own, left_sem.at[col], device(y, core, along(i), side)).start()
-    for j in (1, 7, 2, 6, 3, 5, 4):
-        send(
-            own, right_ref.at[col], right_sem.at[col], device(lax.rem(y + j, 8), side, y, core)
-        ).start()
-    stays = jnp.logical_and(z == y, side == core)
     keep = pltpu.make_async_copy(own, right_ref.at[col], right_sem.at[col])
-    move = send(own, right_ref.at[col], right_sem.at[col], device(y, side, y, core))
-
-    @pl.when(stays)
-    def _():
-        keep.start()
-
-    @pl.when(jnp.logical_not(stays))
-    def _():
-        move.start()
-
-    for i in (0,) + NEAR_FIRST:
-        if i:
-            slot = along(i) * 2 + side
-            wait_for(left_ref, left_sem, slot)
-            block = left_ref.at[slot]
-            send(block, block, left_sem.at[slot], device(y, core, z, 1 - side)).start()
-        slot = along(i) * 2 + core
+    moves = []
+    for i in range(4):
+        target = parity + 2 * i
+        stays = jnp.logical_and(diagonal, target == y)
+        move = send(own, right_ref.at[col], right_sem.at[col], device(target, side, y, core))
+        pl.when(stays)(keep.start)
+        pl.when(jnp.logical_not(stays))(move.start)
+        moves.append((move, stays))
+
+    def hand_left(i):
+        slot = along(i) * 2 + side
+        wait_for(left_ref, left_sem, slot)
+        block = left_ref.at[slot]
+        send(block, block, left_sem.at[slot], device(y, core, z, 1 - side)).start()
+
+    def hand_right(i):
+        slot = (parity + 2 * i) * 2 + core
         wait_for(right_ref, right_sem, slot)
         block = right_ref.at[slot]
+        for k in range(2):
+            send(block, block, right_sem.at[slot], device(up((1, 7)[i % 2]), k, z, side)).start()
         send(block, block, right_sem.at[slot], device(y, 1 - core, z, side)).start()
+
+    for n, i in enumerate(NEAR_FIRST):
+        hand_left(i)
+        if 2 <= n < 6:
+            hand_right(n - 2)
     for i in (0,) + NEAR_FIRST:
         wait_for(left_ref, left_sem, along(i) * 2 + 1 - side)
-        wait_for(right_ref, right_sem, along(i) * 2 + 1 - core)
+    for i in range(8):
+        pl.when(parity != i % 2)(
+            lambda i=i: wait_for(right_ref, right_sem, i * 2 + core)
+        )
+        wait_for(right_ref, right_sem, i * 2 + 1 - core)
+    staying = [move for move, _ in moves]
     for copy in sent:
-        if copy is not move:
+        if not any(copy is move for move in staying):
             copy.wait_send()
-
-    @pl.when(jnp.logical_not(stays))
-    def _():
-        move.wait_send()
+    for move, stays in moves:
+        pl.when(jnp.logical_not(stays))(move.wait_send)
 
 
 def stack_kernel(left_ref, right_ref, out_ref):
@@ -140,28 +184,30 @@
 
 
 def per_device(records, offsets, live_flags):
-    segment = lax.dynamic_slice_in_dim(records, offsets[0], L, 1)
-    spectra = lax.dot_general(
-        dft_rows(), segment, (((1,), (1,)), ((), ())), preferred_element_type=jnp.float32
-    )
-    channels = records.shape[0]
+    channels, held = records.shape
     vmem = pl.BlockSpec(memory_space=pltpu.VMEM)
+    hbm = pl.BlockSpec(memory_space=pltpu.HBM)
     gathered = jax.ShapeDtypeStruct((WINDOWS, SLOT, channels // 2), jnp.float32)
     left, right = pl.pallas_call(
         gather_kernel,
         out_shape=(gathered, gathered),
-        in_specs=[vmem, vmem],
+        in_specs=[hbm] * 4,
         out_specs=(vmem, vmem),
         scratch_shapes=[
+            pltpu.VMEM((channels, held), jnp.bfloat16),
+            pltpu.VMEM((2 * NB, held), jnp.float32),
+            pltpu.SMEM((1,), jnp.int32),
+            pltpu.VMEM((1, channels), jnp.int32),
+            pltpu.SemaphoreType.DMA((4,)),
             pltpu.SemaphoreType.DMA((31,)),
             pltpu.SemaphoreType.DMA((WINDOWS,)),
             pltpu.SemaphoreType.DMA((WINDOWS,)),
         ],
         compiler_params=pltpu.CompilerParams(
-            collective_id=0, has_side_effects=True, vmem_limit_bytes=8 * 2**20
+            collective_id=0, has_side_effects=True, vmem_limit_bytes=52 * 2**20
         ),
         name="gather_spectra",
-    )(spectra, live_flags.reshape(1, channels))
+    )(records, dft_rows(held), offsets, live_flags.reshape(1, channels))
     left = left.reshape(WINDOWS * SLOT, channels // 2)
     right = right.reshape(WINDOWS * SLOT, channels // 2)
     per_step = 4

time: 37.8 us -> 34.1 us (0.902)
  Pallas kernels: 34.2 us -> 31.5 us
  matrix products: 1.37 us -> 0 us
  local copies, waits for them, and re-layouts: 1.11 us -> 1.68 us
    pallas_call x1, Pallas kernels: 30.8 us -> 28.1 us  [per_device(): pl.pallas_call(gather_kernel, out_shape=(gathered, gathered), in_specs=[h...]
    dot_general x1 -> x0, matrix products: 1.37 us -> none  [per_device(): lax.dot_general(dft_rows(), segment, (((1,), (1,)), ((), ())), preferred_...]
    unnamed x4, local copies, waits for them, and re-layouts: 1.11 us -> 1.68 us
where the time goes in v2:
time: 34.1 us; the launch traced here: 33.9 us
  Pallas kernels  31.5 us (92%)
  local copies, waits for them, and re-layouts  1.68 us (5%)
  between operations  0.67 us (2%)
    pallas_call x1, Pallas kernels, per_device(): pl.pallas_call(gather_kernel, out_shape=(gathered, gathered), in_specs=[h...  28.1 us
    pallas_call x1, Pallas kernels, per_device(): pl.pallas_call(stack_kernel, grid=(16 // per_step,), out_shape=jax.ShapeD...  3.41 us
    unnamed x4, local copies, waits for them, and re-layouts  1.68 us

profile of v2, /device:TPU:1, one launch (start us, length us, event | category | flops | bytes accessed | tf_op | source)
XLA Modules:
  0.0 33.9 jit_solution(15479987370152847487)
XLA Ops:
  0.7 0.0 copy-start
  0.7 1.0 %copy-done = f32[64,1664]{1,0:T(8,128)S(1)} copy-done((f32[64,1664]{1,0:T(8,128)S(1)}, f32[64,1664]{1,0:T(8,128)}, u32[]{:S(2)}) %copy-start) | copy-done | bytes 426008
  1.7 0.0 copy-start.1
  1.7 0.7 %copy-done.1 = s32[256]{0:T(256)S(1)} copy-done((s32[256]{0:T(256)S(1)}, s32[256]{0:T(256)}, u32[]{:S(2)}) %copy-start.1) | copy-done | bytes 1048
  2.3 28.1 %gather_spectra.1 = (f32[16,64,128]{2,1,0:T(8,128)S(1)}, f32[16,64,128]{2,1,0:T(8,128)S(1)}) custom-call(bf16[256,1664]{1,0:T(8,128)(2,1)} %records_hbm.1, f32[64,1664]{1,0:T(8,128)S(1)} %copy-done, s32[1]{0:T(128)S(6)} %copy.5.offsets_hbm, s32[1,256]{1,0:T(1,128)S(1)} %bitcast.5), custom_call_target="tpu_custom_call" | custom-call | tf_op jit(solution)/shard_map/gather_spectra/pallas_call | solution.py:191
  30.5 3.4 %stack_windows.1 = bf16[16,2,256,256]{3,2,1,0:T(8,128)(2,1)} custom-call(f32[1024,128]{1,0:T(8,128)S(1)} %bitcast.3, f32[1024,128]{1,0:T(8,128)S(1)} %bitcast.4), custom_call_target="tpu_custom_call" | custom-call | tf_op jit(solution)/shard_map/stack_windows/pallas_call | solution.py:214
Async XLA Ops:
  0.7 1.0 %copy-start = (f32[64,1664]{1,0:T(8,128)S(1)}, f32[64,1664]{1,0:T(8,128)}, u32[]{:S(2)}) copy-start(f32[64,1664]{1,0:T(8,128)} %constant.12.table_hbm) | copy-start | bytes 1277956
  1.7 0.7 %copy-start.1 = (s32[256]{0:T(256)S(1)}, s32[256]{0:T(256)}, u32[]{:S(2)}) copy-start(s32[256]{0:T(256)} %param.6) | copy-start | bytes 3076

commit v3 on v2

--- a/solution.py
+++ b/solution.py
@@ -160,27 +160,36 @@
         pl.when(jnp.logical_not(stays))(move.wait_send)
 
 
-def stack_kernel(left_ref, right_ref, out_ref):
-    step = pl.program_id(0)
-    for k in range(out_ref.shape[0]):
-        first = (step * out_ref.shape[0] + k) * 2
-
-        def rows(ref, part):
-            return jnp.concatenate(
-                [ref[pl.ds(first + part + h * 32, WINDOWS, stride=SLOT), :] for h in (0, 1)],
-                axis=1,
-            )
-
-        real, imag = rows(right_ref, 0), rows(right_ref, 1)
-        left = jnp.concatenate([rows(left_ref, 0), rows(left_ref, 1)], axis=0)
-        left = left.astype(jnp.bfloat16)
+def stack_kernel(left_ref, right_ref, out_hbm, ready_ref, store_sem):
+    def store(first):
+        block = pl.ds(first, 2)
+        return pltpu.make_async_copy(
+            ready_ref.at[block], out_hbm.at[block], store_sem.at[first // 2]
+        )
+
+    def rows(ref, f, part):
+        return jnp.concatenate(
+            [ref[pl.ds(2 * f + part + h * 32, WINDOWS, stride=SLOT), :] for h in (0, 1)], axis=1
+        )
+
+    def stack(f):
+        left = jnp.concatenate([rows(left_ref, f, 0), rows(left_ref, f, 1)], axis=0)
+        left = (left * (1.0 / WINDOWS)).astype(jnp.bfloat16)
+        real, imag = rows(right_ref, f, 0), rows(right_ref, f, 1)
         straight = jnp.concatenate([real, imag], axis=0).astype(jnp.bfloat16)
         turned = jnp.concatenate([-imag, real], axis=0).astype(jnp.bfloat16)
         for part, other in enumerate((straight, turned)):
             total = lax.dot_general(
                 left, other, (((0,), (0,)), ((), ())), preferred_element_type=jnp.float32
             )
-            out_ref[k, part] = (total * (1.0 / WINDOWS)).astype(out_ref.dtype)
+            ready_ref[f, part] = total.astype(ready_ref.dtype)
+
+    for f in range(16):
+        stack(f)
+        if f % 2 == 2 - 1:
+            store(f + 1 - 2).start()
+    for first in range(0, 16, 2):
+        store(first).wait()
 
 
 def per_device(records, offsets, live_flags):
@@ -204,19 +213,27 @@
             pltpu.SemaphoreType.DMA((WINDOWS,)),
         ],
         compiler_params=pltpu.CompilerParams(
-            collective_id=0, has_side_effects=True, vmem_limit_bytes=52 * 2**20
+            collective_id=0, has_side_effects=True, vmem_limit_bytes=12 * 2**20
         ),
         name="gather_spectra",
-    )(records, dft_rows(held), offsets, live_flags.reshape(1, channels))
+    )(
+        pltpu.with_memory_space_constraint(records, pltpu.HBM),
+        pltpu.with_memory_space_constraint(dft_rows(held), pltpu.HBM),
+        offsets,
+        pltpu.with_memory_space_constraint(live_flags.reshape(1, channels), pltpu.HBM),
+    )
     left = left.reshape(WINDOWS * SLOT, channels // 2)
     right = right.reshape(WINDOWS * SLOT, channels // 2)
-    per_step = 4
+    shape = (16, 2, channels, channels)
     return pl.pallas_call(
         stack_kernel,
-        grid=(16 // per_step,),
-        out_shape=jax.ShapeDtypeStruct((16, 2, channels, channels), jnp.bfloat16),
+        out_shape=jax.ShapeDtypeStruct(shape, jnp.bfloat16),
         in_specs=[vmem, vmem],
-        out_specs=pl.BlockSpec((per_step, 2, channels, channels), lambda i: (i, 0, 0, 0)),
+        out_specs=pl.BlockSpec(memory_space=pltpu.HBM),
+        scratch_shapes=[
+            pltpu.VMEM(shape, jnp.bfloat16),
+            pltpu.SemaphoreType.DMA((8,)),
+        ],
         compiler_params=pltpu.CompilerParams(vmem_limit_bytes=16 * 2**20),
         name="stack_windows",
     )(left, right)

time: 34.1 us -> 31.4 us (0.921)
  local copies, waits for them, and re-layouts: 1.68 us -> 0 us
  Pallas kernels: 31.5 us -> 30.6 us
    unnamed x4 -> x0, local copies, waits for them, and re-layouts: 1.68 us -> none
    pallas_call x1, Pallas kernels: 3.41 us -> 2.42 us  [per_device(): pl.pallas_call(stack_kernel, out_shape=jax.ShapeDtypeStruct(shape, jnp.bf...]
where the time goes in v3:
time: 31.4 us; the launch traced here: 31.2 us
  Pallas kernels  30.6 us (97%)
  between operations  0.66 us (2%)
    pallas_call x1, Pallas kernels, per_device(): pl.pallas_call(gather_kernel, out_shape=(gathered, gathered), in_specs=[h...  28.1 us
    pallas_call x1, Pallas kernels, per_device(): pl.pallas_call(stack_kernel, out_shape=jax.ShapeDtypeStruct(shape, jnp.bf...  2.42 us

profile of v3, /device:TPU:1, one launch (start us, length us, event | category | flops | bytes accessed | tf_op | source)
XLA Modules:
  0.0 31.2 jit_solution(2009460913256189701)
XLA Ops:
  0.7 28.1 %gather_spectra.1 = (f32[16,64,128]{2,1,0:T(8,128)S(1)}, f32[16,64,128]{2,1,0:T(8,128)S(1)}) custom-call(bf16[256,1664]{1,0:T(8,128)(2,1)} %records_hbm.1, f32[64,1664]{1,0:T(8,128)} %constant.12.table_hbm, s32[1]{0:T(128)S(6)} %copy.5.offsets_hbm, s32[1,256]{1,0:T(1,128)} %bitcast.5), custom_call_target="tpu_custom_call" | custom-call | tf_op jit(solution)/shard_map/gather_spectra/pallas_call | solution.py:200
  28.8 2.4 %stack_windows.1 = bf16[16,2,256,256]{3,2,1,0:T(8,128)(2,1)} custom-call(f32[1024,128]{1,0:T(8,128)S(1)} %bitcast.3, f32[1024,128]{1,0:T(8,128)S(1)} %bitcast.4), custom_call_target="tpu_custom_call" | custom-call | tf_op jit(solution)/shard_map/stack_windows/pallas_call | solution.py:228

commit v4 on v3

--- a/solution.py
+++ b/solution.py
@@ -30,7 +30,7 @@
 
 def gather_kernel(
     records_hbm, table_hbm, offsets_hbm, live_hbm, left_ref, right_ref,
-    records_ref, table_ref, offsets_ref, live_ref, load_sem, send_sem, left_sem, right_sem,
+    records_ref, table_ref, offsets_ref, live_ref, load_sem, send_sem, left_sem, right_sem, opposite_sem,
 ):
     row, col, half = lax.axis_index("row"), lax.axis_index("col"), lax.axis_index("bin")
     y, core = row // 2, row % 2
@@ -115,7 +115,7 @@
 
     own = left_ref.at[col]
     send(own, own, left_sem.at[col], device(y, core, z, 1 - side)).start()
-    for i in NEAR_FIRST:
+    for i in (1, 7, 3, 5, 2, 6):
         send(own, own, left_sem.at[col], device(y, core, along(i), side)).start()
     keep = pltpu.make_async_copy(own, right_ref.at[col], right_sem.at[col])
     moves = []
@@ -127,24 +127,51 @@
         pl.when(jnp.logical_not(stays))(move.start)
         moves.append((move, stays))
 
+    lefts, rights = {}, {}
+    for i in NEAR_FIRST:
+        slot = along(i) * 2 + side
+        block = left_ref.at[slot]
+        lefts[i] = slot, send(block, block, left_sem.at[slot], device(y, core, z, 1 - side))
+    for i in range(4):
+        slot = (parity + 2 * i) * 2 + core
+        block = right_ref.at[slot]
+        onward = [
+            send(block, block, right_sem.at[slot], device(up((1, 7)[i % 2]), k, z, side))
+            for k in range(2)
+        ]
+        onward.append(send(block, block, right_sem.at[slot], device(y, 1 - core, z, side)))
+        rights[i] = slot, onward
+
+    def opposite(i):
+        slot = along(i) * 2 + side
+        block = left_ref.at[slot]
+        return pltpu.make_async_remote_copy(
+            src_ref=block,
+            dst_ref=block,
+            send_sem=opposite_sem,
+            recv_sem=left_sem.at[slot],
+            device_id=device(y, core, along(7 if i == 3 else 1), side),
+            device_id_type=MESH,
+        )
+
     def hand_left(i):
-        slot = along(i) * 2 + side
+        slot, copy = lefts[i]
         wait_for(left_ref, left_sem, slot)
-        block = left_ref.at[slot]
-        send(block, block, left_sem.at[slot], device(y, core, z, 1 - side)).start()
+        if i in (3, 5):
+            pl.when(core == (i == 3))(opposite(i).start)
+        copy.start()
 
     def hand_right(i):
-        slot = (parity + 2 * i) * 2 + core
+        slot, onward = rights[i]
         wait_for(right_ref, right_sem, slot)
-        block = right_ref.at[slot]
-        for k in range(2):
-            send(block, block, right_sem.at[slot], device(up((1, 7)[i % 2]), k, z, side)).start()
-        send(block, block, right_sem.at[slot], device(y, 1 - core, z, side)).start()
-
-    for n, i in enumerate(NEAR_FIRST):
-        hand_left(i)
-        if 2 <= n < 6:
-            hand_right(n - 2)
+        for copy in onward:
+            copy.start()
+
+    def hand_on(order):
+        for name in order.split():
+            (hand_left if name[0] == "L" else hand_right)(int(name[1]))
+
+    hand_on("L1 L7 L5 L3 R0 L2 R1 L6 R2 L4 R3")
     for i in (0,) + NEAR_FIRST:
         wait_for(left_ref, left_sem, along(i) * 2 + 1 - side)
     for i in range(8):
@@ -158,6 +185,7 @@
             copy.wait_send()
     for move, stays in moves:
         pl.when(jnp.logical_not(stays))(move.wait_send)
+    opposite(3).wait_send()
 
 
 def stack_kernel(left_ref, right_ref, out_hbm, ready_ref, store_sem):
@@ -211,6 +239,7 @@
             pltpu.SemaphoreType.DMA((31,)),
             pltpu.SemaphoreType.DMA((WINDOWS,)),
             pltpu.SemaphoreType.DMA((WINDOWS,)),
+            pltpu.SemaphoreType.DMA,
         ],
         compiler_params=pltpu.CompilerParams(
             collective_id=0, has_side_effects=True, vmem_limit_bytes=12 * 2**20

time: 31.4 us -> 31.2 us (level)
  no operation moved by 1% of the time
where the time goes in v4:
time: 31.2 us; the launch traced here: 31 us
  Pallas kernels  30.3 us (97%)
  between operations  0.66 us (2%)
    pallas_call x1, Pallas kernels, per_device(): pl.pallas_call(gather_kernel, out_shape=(gathered, gathered), in_specs=[h...  27.9 us
    pallas_call x1, Pallas kernels, per_device(): pl.pallas_call(stack_kernel, out_shape=jax.ShapeDtypeStruct(shape, jnp.bf...  2.42 us

profile of v4, /device:TPU:1, one launch (start us, length us, event | category | flops | bytes accessed | tf_op | source)
XLA Modules:
  0.0 31.0 jit_solution(3812955029373838642)
XLA Ops:
  0.7 27.9 %gather_spectra.1 = (f32[16,64,128]{2,1,0:T(8,128)S(1)}, f32[16,64,128]{2,1,0:T(8,128)S(1)}) custom-call(bf16[256,1664]{1,0:T(8,128)(2,1)} %records_hbm.1, f32[64,1664]{1,0:T(8,128)} %constant.12.table_hbm, s32[1]{0:T(128)S(6)} %copy.5.offsets_hbm, s32[1,256]{1,0:T(1,128)} %bitcast.5), custom_call_target="tpu_custom_call" | custom-call | tf_op jit(solution)/shard_map/gather_spectra/pallas_call | solution.py:228
  28.6 2.4 %stack_windows.1 = bf16[16,2,256,256]{3,2,1,0:T(8,128)(2,1)} custom-call(f32[1024,128]{1,0:T(8,128)S(1)} %bitcast.3, f32[1024,128]{1,0:T(8,128)S(1)} %bitcast.4), custom_call_target="tpu_custom_call" | custom-call | tf_op jit(solution)/shard_map/stack_windows/pallas_call | solution.py:257

commit v5 on v4

--- a/solution.py
+++ b/solution.py
@@ -114,9 +114,6 @@
         pltpu.make_async_copy(ref.at[slot], ref.at[slot], sem.at[slot]).wait()
 
     own = left_ref.at[col]
-    send(own, own, left_sem.at[col], device(y, core, z, 1 - side)).start()
-    for i in (1, 7, 3, 5, 2, 6):
-        send(own, own, left_sem.at[col], device(y, core, along(i), side)).start()
     keep = pltpu.make_async_copy(own, right_ref.at[col], right_sem.at[col])
     moves = []
     for i in range(4):
@@ -127,6 +124,9 @@
         pl.when(jnp.logical_not(stays))(move.start)
         moves.append((move, stays))
 
+    send(own, own, left_sem.at[col], device(y, core, z, 1 - side)).start()
+    for i in (1, 7, 3, 5, 2, 6):
+        send(own, own, left_sem.at[col], device(y, core, along(i), side)).start()
     lefts, rights = {}, {}
     for i in NEAR_FIRST:
         slot = along(i) * 2 + side

time: 31.2 us -> 32.6 us (1.045)
  Pallas kernels: 30.3 us -> 31.8 us
    pallas_call x1, Pallas kernels: 27.9 us -> 29.4 us  [per_device(): pl.pallas_call(gather_kernel, out_shape=(gathered, gathered), in_specs=[h...]
where the time goes in v5:
time: 32.6 us; the launch traced here: 32.5 us
  Pallas kernels  31.8 us (98%)
  between operations  0.66 us (2%)
    pallas_call x1, Pallas kernels, per_device(): pl.pallas_call(gather_kernel, out_shape=(gathered, gathered), in_specs=[h...  29.4 us
    pallas_call x1, Pallas kernels, per_device(): pl.pallas_call(stack_kernel, out_shape=jax.ShapeDtypeStruct(shape, jnp.bf...  2.42 us

profile of v5, /device:TPU:1, one launch (start us, length us, event | category | flops | bytes accessed | tf_op | source)
XLA Modules:
  0.0 32.5 jit_solution(15879238786702960435)
XLA Ops:
  0.7 29.4 %gather_spectra.1 = (f32[16,64,128]{2,1,0:T(8,128)S(1)}, f32[16,64,128]{2,1,0:T(8,128)S(1)}) custom-call(bf16[256,1664]{1,0:T(8,128)(2,1)} %records_hbm.1, f32[64,1664]{1,0:T(8,128)} %constant.12.table_hbm, s32[1]{0:T(128)S(6)} %copy.5.offsets_hbm, s32[1,256]{1,0:T(1,128)} %bitcast.5), custom_call_target="tpu_custom_call" | custom-call | tf_op jit(solution)/shard_map/gather_spectra/pallas_call | solution.py:228
  30.1 2.4 %stack_windows.1 = bf16[16,2,256,256]{3,2,1,0:T(8,128)(2,1)} custom-call(f32[1024,128]{1,0:T(8,128)S(1)} %bitcast.3, f32[1024,128]{1,0:T(8,128)S(1)} %bitcast.4), custom_call_target="tpu_custom_call" | custom-call | tf_op jit(solution)/shard_map/stack_windows/pallas_call | solution.py:257
